TPU v7x, 32 devices: a whole 2x2x4 slice. The times are simulated.
32 devices in a mesh: pipe: 8 (over y, x, core), seq: 4 (over z).
Axes of the slice: x: 2, y: 2, z: 4, core: 2. Of those that a mesh axis runs over, the one named last changes fastest.
Arguments:
- layer_input: bfloat16 [8, 256, 2, 1536], P('pipe', 'seq'), may hold values from -1.5 to 1.5
- grad_out: bfloat16 [8, 256, 2, 1536], P('pipe', 'seq'), may hold values from -6 to 6
- queries: bfloat16 [8, 256, 2, 768], P('pipe', 'seq'), may hold values from -8 to 8
- keys_saved: bfloat16 [8, 256, 2, 768], P('pipe', 'seq'), may hold values from -8 to 8
- values_saved: bfloat16 [8, 256, 2, 768], P('pipe', 'seq'), may hold values from -6 to 6
- out_weight: bfloat16 [8, 768, 1536], P('pipe'), may hold values from -0.15625 to 0.15625
- qkv_weight: bfloat16 [8, 1536, 2304], P('pipe'), may hold values from -0.125 to 0.125
- ln_gain: bfloat16 [8, 1536], P('pipe'), may hold values from 0.099609375 to 1.8984375
- lengths: int32 [8, 2], P('pipe'), may hold values from 33 to 256
Outputs:
- passed: bfloat16 [8, 256, 2, 1536], P('pipe', 'seq')
All inputs are finite; a program needn't handle non-finite values.
Results may differ from a plain program's by a relative error of at most 0.0063.
Values may be sent and summed in bfloat16 or wider, within the bound.
A program may use at most 64 MiB of HBM per device.

v0:
```python
import jax
import jax.numpy as jnp
from jax import lax
from jax.sharding import PartitionSpec as P

HEADS_W = 12
HD = 64


def passed_along(block, axis, distance):
    devices = range(lax.axis_size(axis))
    route = [((i - distance) % len(devices), i) for i in devices]
    return lax.ppermute(block, axis, route)


def norm_backward(inputs, norm_gain, upstream):
    row_mean = jnp.mean(inputs, axis=-1, keepdims=True)
    centred = inputs - row_mean
    row_var = jnp.mean(centred * centred, axis=-1, keepdims=True)
    inv_std = lax.rsqrt(row_var + 1e-05)
    normed = centred * inv_std
    scaled = upstream * norm_gain
    return inv_std * (
        scaled
        - jnp.mean(scaled, axis=-1, keepdims=True)
        - normed * jnp.mean(scaled * normed, axis=-1, keepdims=True)
    )


def attend(query_heads, key_heads, value_heads, grad_heads, key_lengths):
    length = query_heads.shape[0]
    pair_count = query_heads.shape[1] // HD
    factor = HD ** (-0.5)
    query_split = query_heads.reshape(length, pair_count, HD)
    key_split = key_heads.reshape(length, pair_count, HD)
    value_split = value_heads.reshape(length, pair_count, HD)
    grad_split = grad_heads.reshape(length, pair_count, HD)
    block = 512 if length % 512 == 0 else length
    usable = jnp.arange(length)[None, None, :] < key_lengths[:, None, None]

    def one_block(carried, block_index):
        key_acc, value_acc = carried
        query_block = lax.dynamic_slice_in_dim(query_split, block_index * block, block, 0)
        grad_block = lax.dynamic_slice_in_dim(grad_split, block_index * block, block, 0)
        scores = (
            jnp.einsum("qph,kph->pqk", query_block, key_split, preferred_element_type=jnp.float32)
            * factor
        )
        masked = jnp.where(usable, scores, -jnp.inf)
        row_peak = jnp.max(masked, axis=-1, keepdims=True)
        exp_terms = jnp.exp(masked - row_peak)
        prob_full = exp_terms / jnp.sum(exp_terms, axis=-1, keepdims=True)
        prob_low = prob_full.astype(jnp.bfloat16)
        value_acc = value_acc + jnp.einsum(
            "pqk,qph->kph", prob_low, grad_block, preferred_element_type=jnp.float32
        )
        grad_prob = jnp.einsum(
            "qph,kph->pqk", grad_block, value_split, preferred_element_type=jnp.float32
        )
        row_delta = jnp.sum(prob_full * grad_prob, axis=-1, keepdims=True)
        grad_score = (prob_full * (grad_prob - row_delta)).astype(jnp.bfloat16)
        grad_query = (
            jnp.einsum("pqk,kph->qph", grad_score, key_split, preferred_element_type=jnp.float32)
            * factor
        ).astype(jnp.bfloat16)
        key_acc = key_acc + jnp.einsum(
            "pqk,qph->kph", grad_score, query_block, preferred_element_type=jnp.float32
        )
        return ((key_acc, value_acc), grad_query)

    empty_acc = jnp.zeros((length, pair_count, HD), jnp.float32)
    (key_acc, value_acc), query_blocks = lax.scan(
        one_block, (empty_acc, empty_acc), jnp.arange(length // block)
    )
    grad_query = query_blocks.reshape(length, pair_count * HD)
    grad_key = (key_acc * factor).astype(jnp.bfloat16).reshape(length, pair_count * HD)
    grad_value = value_acc.astype(jnp.bfloat16).reshape(length, pair_count * HD)
    return (grad_query, grad_key, grad_value)


def per_device(
    layer_input,
    grad_out,
    queries,
    keys_saved,
    values_saved,
    out_weight,
    qkv_weight,
    ln_gain,
    lengths,
):
    frames = grad_out.shape[1]
    record_count = grad_out.shape[2]
    feature_count = grad_out.shape[3]
    inner_width = out_weight.shape[1]
    row_count = frames * record_count
    flat_grad = grad_out[0].reshape(row_count, feature_count)
    query_cols = queries[0].reshape(frames, record_count * inner_width)
    key_cols = keys_saved[0].reshape(frames, record_count * inner_width)
    value_cols = values_saved[0].reshape(frames, record_count * inner_width)
    product = lax.dot_general(
        flat_grad, out_weight[0], (((1,), (1,)), ((), ())), preferred_element_type=jnp.float32
    )
    grad_cols = product.astype(jnp.bfloat16).reshape(frames, record_count * inner_width)
    query_heads, key_heads, value_heads, grad_heads = (
        lax.all_to_all(query_cols, "seq", split_axis=1, concat_axis=0, tiled=True),
        lax.all_to_all(key_cols, "seq", split_axis=1, concat_axis=0, tiled=True),
        lax.all_to_all(value_cols, "seq", split_axis=1, concat_axis=0, tiled=True),
        lax.all_to_all(grad_cols, "seq", split_axis=1, concat_axis=0, tiled=True),
    )
    pair_count = query_heads.shape[1] // HD
    pair_ids = lax.axis_index("seq") * pair_count + jnp.arange(pair_count)
    record_ids = pair_ids // HEADS_W
    key_lengths = jnp.sum(
        jnp.where(record_ids[:, None] == jnp.arange(record_count)[None, :], lengths[0][None, :], 0),
        axis=1,
    )
    grad_query, grad_key, grad_value = attend(
        query_heads, key_heads, value_heads, grad_heads, key_lengths
    )
    back_query, back_key, back_value = (
        lax.all_to_all(grad_query, "seq", split_axis=0, concat_axis=1, tiled=True),
        lax.all_to_all(grad_key, "seq", split_axis=0, concat_axis=1, tiled=True),
        lax.all_to_all(grad_value, "seq", split_axis=0, concat_axis=1, tiled=True),
    )
    joined = jnp.concatenate(
        [
            back_query.reshape(row_count, inner_width),
            back_key.reshape(row_count, inner_width),
            back_value.reshape(row_count, inner_width),
        ],
        axis=1,
    )
    grad_normed = lax.dot_general(
        joined, qkv_weight[0], (((1,), (1,)), ((), ())), preferred_element_type=jnp.float32
    )
    inputs = layer_input[0].reshape(row_count, feature_count).astype(jnp.float32)
    branch = norm_backward(inputs, ln_gain[0].astype(jnp.float32)[None, :], grad_normed)
    total = (flat_grad.astype(jnp.float32) + branch).astype(jnp.bfloat16)
    passed = passed_along(total, "pipe", -1)
    return passed.reshape(1, frames, record_count, feature_count)


def solution(mesh):
    placed = (
        P("pipe", "seq", None, None),
        P("pipe", "seq", None, None),
        P("pipe", "seq", None, None),
        P("pipe", "seq", None, None),
        P("pipe", "seq", None, None),
        P("pipe", None, None),
        P("pipe", None, None),
        P("pipe", None),
        P("pipe", None),
    )
    return jax.shard_map(
        per_device,
        mesh=mesh,
        in_specs=placed,
        out_specs=P("pipe", "seq", None, None),
        check_vma=False,
    )
```

profile of v0, /device:TPU:1, one launch (start us, length us, event | category | flops | bytes accessed | tf_op | source)
XLA Modules:
  0.0 99.9 jit_solution(9526014690568722085)
XLA Ops:
  0.0 1.2 %all_to_all.84 = bf16[64,4,384]{2,1,0:T(4,128)(2,1)S(1)} reshape(bf16[1,64,2,768]{3,2,1,0:T(2,128)(2,1)} %param.11) | data formatting | bytes 393216 | tf_op jit(solution)/shard_map/all_to_all | solution.py:106
  1.2 0.7 copy.58
  1.9 5.4 %all-to-all-start = ((bf16[64,4,384]{2,0,1:T(8,128)(2,1)}), bf16[64,4,384]{2,0,1:T(8,128)(2,1)S(1)}, u32[]{:S(2)}, u32[]{:S(2)}) async-start(bf16[64,4,384]{2,0,1:T(8,128)(2,1)} %copy.58), calls=%async_computation | async-start | bytes 393216 | tf_op jit(solution)/shard_map/all_to_all | solution.py:106
  7.3 1.0 %all_to_all.87 = bf16[64,4,384]{2,1,0:T(4,128)(2,1)S(1)} reshape(bf16[1,64,2,768]{3,2,1,0:T(2,128)(2,1)} %param.12) | data formatting | bytes 393216 | tf_op jit(solution)/shard_map/all_to_all | solution.py:107
  8.3 0.7 copy.60
  9.2 3.3 %all-to-all-done = bf16[64,4,384]{2,0,1:T(8,128)(2,1)S(1)} async-done(((bf16[64,4,384]{2,0,1:T(8,128)(2,1)}), bf16[64,4,384]{2,0,1:T(8,128)(2,1)S(1)}, u32[]{:S(2)}, u32[]{:S(2)}) %all-to-all-start) | async-done | bytes 196640 | tf_op jit(solution)/shard_map/all_to_all | solution.py:106
  12.5 4.4 %all-to-all-start.1 = ((bf16[64,4,384]{2,0,1:T(8,128)(2,1)}), bf16[64,4,384]{2,0,1:T(8,128)(2,1)}, u32[]{:S(2)}, u32[]{:S(2)}) async-start(bf16[64,4,384]{2,0,1:T(8,128)(2,1)} %copy.60), calls=%async_computation.1 | async-start | bytes 393216 | tf_op jit(solution)/shard_map/all_to_all | solution.py:107
  16.9 0.9 fusion.12
  18.0 0.7 copy.62
  18.7 1.0 %all_to_all.93 = bf16[64,4,384]{2,1,0:T(4,128)(2,1)S(1)} reshape(bf16[1,64,2,768]{3,2,1,0:T(2,128)(2,1)} %param.13) | data formatting | bytes 393216 | tf_op jit(solution)/shard_map/all_to_all | solution.py:108
  19.7 0.7 copy.64
  20.4 1.7 %all-to-all-done.1 = bf16[64,4,384]{2,0,1:T(8,128)(2,1)} async-done(((bf16[64,4,384]{2,0,1:T(8,128)(2,1)}), bf16[64,4,384]{2,0,1:T(8,128)(2,1)}, u32[]{:S(2)}, u32[]{:S(2)}) %all-to-all-start.1) | async-done | bytes 196640 | tf_op jit(solution)/shard_map/all_to_all | solution.py:107
  22.1 3.4 %all-to-all-start.2 = ((bf16[64,4,384]{2,0,1:T(8,128)(2,1)}), bf16[64,4,384]{2,0,1:T(8,128)(2,1)S(1)}, u32[]{:S(2)}, u32[]{:S(2)}) async-start(bf16[64,4,384]{2,0,1:T(8,128)(2,1)} %copy.62), calls=%async_computation.2 | async-start | bytes 393216 | tf_op jit(solution)/shard_map/all_to_all | solution.py:109
  25.6 4.9 %all-to-all-done.2 = bf16[64,4,384]{2,0,1:T(8,128)(2,1)S(1)} async-done(((bf16[64,4,384]{2,0,1:T(8,128)(2,1)}), bf16[64,4,384]{2,0,1:T(8,128)(2,1)S(1)}, u32[]{:S(2)}, u32[]{:S(2)}) %all-to-all-start.2) | async-done | bytes 196640 | tf_op jit(solution)/shard_map/all_to_all | solution.py:109
  30.5 4.0 %all-to-all-start.3 = ((bf16[64,4,384]{2,0,1:T(8,128)(2,1)}), bf16[64,4,384]{2,0,1:T(8,128)(2,1)}, u32[]{:S(2)}, u32[]{:S(2)}) async-start(bf16[64,4,384]{2,0,1:T(8,128)(2,1)} %copy.64), calls=%async_computation.3 | async-start | bytes 393216 | tf_op jit(solution)/shard_map/all_to_all | solution.py:108
  34.9 0.6 broadcast_multiply_fusion
  36.1 1.2 %copy.61 = bf16[4,64,384]{1,0,2:T(4,128)(2,1)S(1)} copy(bf16[4,64,384]{2,1,0:T(8,128)(2,1)} %bitcast.2) | data formatting | bytes 393216 | tf_op jit(solution)/shard_map/all_to_all | solution.py:107
  37.6 1.2 %copy.63 = bf16[4,64,384]{1,0,2:T(4,128)(2,1)S(1)} copy(bf16[4,64,384]{2,1,0:T(8,128)(2,1)} %bitcast.52) | data formatting | bytes 393216 | tf_op jit(solution)/shard_map/all_to_all | solution.py:109
  38.8 1.0 reshape.146
  39.8 1.2 %copy.65 = bf16[4,64,384]{1,0,2:T(4,128)(2,1)S(1)} copy(bf16[4,64,384]{2,1,0:T(8,128)(2,1)} %bitcast.5) | data formatting | bytes 393216 | tf_op jit(solution)/shard_map/all_to_all | solution.py:108
  41.0 1.0 reshape.147
  41.9 1.8 %fusion.30 = (f32[6,256]{1,0:T(8,128)S(1)}, f32[6,256,256]{1,2,0:T(8,128)}) fusion(bf16[256,6,64]{0,2,1:T(8,128)(2,1)S(1)} %reshape.144, bf16[256,6,64]{0,2,1:T(8,128)(2,1)S(1)} %reshape.145, pred[6,256]{1,0:T(8,128)(4,1)S(1)} %iota_compare_fusion), kind=kOutput, calls=%fused_computation.46 | convolution fusion | flops 51904768 | bytes 1973760 | tf_op jit(solution)/shard_map/while/body/eval_jaxpr/sub | solution.py:51
  43.8 1.9 %multiply_reduce_fusion = (f32[6,256]{1,0:T(8,128)S(1)}, f32[6,256,256]{1,2,0:T(8,128)S(1)}) fusion(f32[6,256,256]{1,2,0:T(8,128)} %get-tuple-element.24, f32[6,256]{1,0:T(8,128)S(1)} %get-tuple-element.23, bf16[256,6,64]{0,2,1:T(8,128)(2,1)S(1)} %copy-done.12, bf16[256,6,64]{0,2,1:T(8,128)(2,1)S(1)} %copy-done.13), kind=kOutput, calls=%fused_computation.8 | convolution fusion | flops 51509760 | bytes 3551232 | tf_op jit(solution)/shard_map/while/body/eval_jaxpr/qph,kph->pqk/dot_general | solution.py:57
  46.0 0.9 copy-done.1
  47.4 0.9 copy.67
  48.3 4.5 %all-to-all-start.4 = ((bf16[4,64,384]{2,1,0:T(8,128)(2,1)}), bf16[4,64,384]{2,1,0:T(8,128)(2,1)}, u32[]{:S(2)}, u32[]{:S(2)}) async-start(bf16[4,64,384]{2,1,0:T(8,128)(2,1)} %copy.67), calls=%async_computation.4 | async-start | bytes 393216 | tf_op jit(solution)/shard_map/all_to_all | solution.py:122
  52.8 1.2 %multiply_reduce_fusion.2 = f32[64,2]{1,0:T(8,128)} fusion(f32[64,2]{1,0:T(8,128)S(1)} %copy-done.11, bf16[1,64,2,1536]{3,2,1,0:T(2,128)(2,1)S(1)} %copy-done.2), kind=kLoop, calls=%fused_computation.25 | loop fusion | flops 786304 | bytes 394240 | tf_op jit(solution)/shard_map/reduce_sum | solution.py:19
  54.0 0.6 div.42
  54.8 2.2 %fusion.17 = bf16[256,6,64]{0,2,1:T(8,128)(2,1)} fusion(bf16[6,256,256]{1,2,0:T(8,128)(2,1)} %copy-done.1, bf16[256,6,64]{0,2,1:T(8,128)(2,1)} %copy-done.6), kind=kOutput, calls=%fused_computation.19 | convolution fusion | flops 50528256 | bytes 1179648 | tf_op jit(solution)/shard_map/while/body/eval_jaxpr/pqk,qph->kph/dot_general | solution.py:66
  57.0 1.2 %all_to_all.99 = bf16[4,64,384]{1,0,2:T(4,128)(2,1)S(1)} reshape(bf16[256,6,64]{0,2,1:T(8,128)(2,1)} %fusion.17) | data formatting | bytes 393216 | tf_op jit(solution)/shard_map/all_to_all | solution.py:123
  58.1 0.9 copy.70
  59.1 4.5 %all-to-all-start.5 = ((bf16[4,64,384]{2,1,0:T(8,128)(2,1)}), bf16[4,64,384]{2,1,0:T(8,128)(2,1)}, u32[]{:S(2)}, u32[]{:S(2)}) async-start(bf16[4,64,384]{2,1,0:T(8,128)(2,1)} %copy.70), calls=%async_computation.5 | async-start | bytes 393216 | tf_op jit(solution)/shard_map/all_to_all | solution.py:123
  63.6 2.6 %fusion.15 = bf16[256,6,64]{0,2,1:T(8,128)(2,1)} fusion(bf16[256,6,64]{0,2,1:T(8,128)(2,1)} %reshape.146, f32[6,256,256]{1,2,0:T(8,128)} %get-tuple-element.24, f32[6,256]{1,0:T(8,128)S(1)} %get-tuple-element.23), kind=kOutput, calls=%fused_computation.17 | convolution fusion | flops 51216384 | bytes 1972224 | tf_op jit(solution)/shard_map/while/body/eval_jaxpr/pqk,qph->kph/dot_general | solution.py:54
  66.2 1.2 %all_to_all.102 = bf16[4,64,384]{1,0,2:T(4,128)(2,1)S(1)} reshape(bf16[256,6,64]{0,2,1:T(8,128)(2,1)} %fusion.15) | data formatting | bytes 393216 | tf_op jit(solution)/shard_map/all_to_all | solution.py:124
  67.3 0.9 copy.73
  68.3 0.6 all-to-all-done.5
  68.8 4.0 %all-to-all-start.6 = ((bf16[4,64,384]{2,1,0:T(8,128)(2,1)}), bf16[4,64,384]{2,1,0:T(8,128)(2,1)S(1)}, u32[]{:S(2)}, u32[]{:S(2)}) async-start(bf16[4,64,384]{2,1,0:T(8,128)(2,1)} %copy.73), calls=%async_computation.6 | async-start | bytes 393216 | tf_op jit(solution)/shard_map/all_to_all | solution.py:124
  72.8 0.8 add_rsqrt_fusion
  73.6 0.6 rsqrt.12
  74.2 1.1 %copy.68 = bf16[64,4,384]{2,1,0:T(4,128)(2,1)S(1)} copy(bf16[64,4,384]{2,0,1:T(8,128)(2,1)} %bitcast.7) | data formatting | bytes 393216 | tf_op jit(solution)/shard_map/all_to_all | solution.py:122
  75.3 0.8 reshape.148
  76.1 1.1 %copy.71 = bf16[64,4,384]{2,1,0:T(4,128)(2,1)S(1)} copy(bf16[64,4,384]{2,0,1:T(8,128)(2,1)} %bitcast.9) | data formatting | bytes 393216 | tf_op jit(solution)/shard_map/all_to_all | solution.py:123
  77.2 0.8 reshape.149
  78.3 5.8 %fusion.29 = (f32[128]{0:T(128)S(1)}, f32[128]{0:T(128)S(1)}, f32[128,1536]{1,0:T(8,128)S(1)}) fusion(f32[128]{0:T(128)S(1)} %copy-done.16, f32[128,1536]{1,0:T(8,128)S(1)} %reshape.153, f32[128]{0:T(128)} %div.42, f32[1536]{0:T(1024)S(1)} %convert_reduce_fusion.1, bf16[1,1536,2304]{2,1,0:T(8,128)(2,1)} %param.15, bf16[128,768]{1,0:T(8,128)(2,1)S(1)} %reshape.150, ...), kind=kOutput, calls=%fused_computation.45 | convolution fusion | flops 908918528 | bytes 9248768 | tf_op jit(solution)/shard_map/dot_general | solution.py:134
  84.1 0.4 add_convert_fusion
  84.5 7.9 %collective-permute-start = (bf16[128,1536]{1,0:T(8,128)(2,1)S(1)}, bf16[128,1536]{1,0:T(8,128)(2,1)S(1)}, u32[]{:S(2)}, u32[]{:S(2)}) collective-permute-start(bf16[128,1536]{1,0:T(8,128)(2,1)S(1)} %add_convert_fusion), channel_id=1, source_target_pairs={{4,0},{8,4},{12,8},{16,12},{20,16},{24,20},{28,24},{0,28},{5,1},{9... | collective-permute-start | bytes 1179656 | tf_op jit(solution)/shard_map/ppermute | solution.py:13
  92.4 6.6 %collective-permute-done = bf16[128,1536]{1,0:T(8,128)(2,1)S(1)} collective-permute-done((bf16[128,1536]{1,0:T(8,128)(2,1)S(1)}, bf16[128,1536]{1,0:T(8,128)(2,1)S(1)}, u32[]{:S(2)}, u32[]{:S(2)}) %collective-permute-start) | collective-permute-done | bytes 393248 | tf_op jit(solution)/shard_map/ppermute | solution.py:13
  99.0 0.9 reshape.151
  (55 shorter events, 2.9 us)
Async XLA Ops:
  0.0 16.9 %copy-start = (bf16[1,768,1536]{2,1,0:T(8,128)(2,1)S(1)}, bf16[1,768,1536]{2,1,0:T(8,128)(2,1)}, u32[]{:S(2)}) copy-start(bf16[1,768,1536]{2,1,0:T(8,128)(2,1)} %param.14) | copy-start | bytes 7077892
  0.0 9.0 %copy-start.10 = (bf16[1,64,2,1536]{3,2,1,0:T(2,128)(2,1)S(1)}, bf16[1,64,2,1536]{3,2,1,0:T(2,128)(2,1)}, u32[]{:S(2)}) copy-start(bf16[1,64,2,1536]{3,2,1,0:T(2,128)(2,1)} %param.10) | copy-start | bytes 1179652
  1.9 10.6 %all-to-all-start = ((bf16[64,4,384]{2,0,1:T(8,128)(2,1)}), bf16[64,4,384]{2,0,1:T(8,128)(2,1)S(1)}, u32[]{:S(2)}, u32[]{:S(2)}) async-start(bf16[64,4,384]{2,0,1:T(8,128)(2,1)} %copy.58), calls=%async_computation | async-start | bytes 393216 | tf_op jit(solution)/shard_map/all_to_all | solution.py:106
  9.1 8.6 %copy-start.3 = (bf16[128,1536]{1,0:T(8,128)(2,1)}, bf16[128,1536]{1,0:T(8,128)(2,1)S(1)}, u32[]{:S(2)}) copy-start(bf16[128,1536]{1,0:T(8,128)(2,1)S(1)} %reshape_squeeze.2) | copy-start | bytes 1179652
  12.5 4.4 %copy-start.7 = (bf16[64,4,384]{2,0,1:T(8,128)(2,1)}, bf16[64,4,384]{2,0,1:T(8,128)(2,1)S(1)}, u32[]{:S(2)}) copy-start(bf16[64,4,384]{2,0,1:T(8,128)(2,1)S(1)} %all-to-all-done) | copy-start | bytes 589828
  12.5 9.6 %all-to-all-start.1 = ((bf16[64,4,384]{2,0,1:T(8,128)(2,1)}), bf16[64,4,384]{2,0,1:T(8,128)(2,1)}, u32[]{:S(2)}, u32[]{:S(2)}) async-start(bf16[64,4,384]{2,0,1:T(8,128)(2,1)} %copy.60), calls=%async_computation.1 | async-start | bytes 393216 | tf_op jit(solution)/shard_map/all_to_all | solution.py:107
  17.8 7.7 %copy-start.17 = (s32[1,2]{1,0:T(1,128)S(1)}, s32[1,2]{1,0:T(1,128)}, u32[]{:S(2)}) copy-start(s32[1,2]{1,0:T(1,128)} %param.17) | copy-start | bytes 28
  17.8 16.7 %copy-start.2 = (bf16[1,64,2,1536]{3,2,1,0:T(2,128)(2,1)S(1)}, bf16[1,64,2,1536]{3,2,1,0:T(2,128)(2,1)}, u32[]{:S(2)}) copy-start(bf16[1,64,2,1536]{3,2,1,0:T(2,128)(2,1)} %param.9) | copy-start | bytes 1179652
  17.9 17.6 %copy-start.8 = (bf16[64,4,384]{2,0,1:T(8,128)(2,1)S(1)}, bf16[64,4,384]{2,0,1:T(8,128)(2,1)}, u32[]{:S(2)}) copy-start(bf16[64,4,384]{2,0,1:T(8,128)(2,1)} %copy-done.7) | copy-start | bytes 589828
  22.1 8.4 %all-to-all-start.2 = ((bf16[64,4,384]{2,0,1:T(8,128)(2,1)}), bf16[64,4,384]{2,0,1:T(8,128)(2,1)S(1)}, u32[]{:S(2)}, u32[]{:S(2)}) async-start(bf16[64,4,384]{2,0,1:T(8,128)(2,1)} %copy.62), calls=%async_computation.2 | async-start | bytes 393216 | tf_op jit(solution)/shard_map/all_to_all | solution.py:109
  30.5 5.0 %copy-start.9 = (bf16[64,4,384]{2,0,1:T(8,128)(2,1)}, bf16[64,4,384]{2,0,1:T(8,128)(2,1)S(1)}, u32[]{:S(2)}) copy-start(bf16[64,4,384]{2,0,1:T(8,128)(2,1)S(1)} %all-to-all-done.2) | copy-start | bytes 589828
  30.5 9.2 %all-to-all-start.3 = ((bf16[64,4,384]{2,0,1:T(8,128)(2,1)}), bf16[64,4,384]{2,0,1:T(8,128)(2,1)}, u32[]{:S(2)}, u32[]{:S(2)}) async-start(bf16[64,4,384]{2,0,1:T(8,128)(2,1)} %copy.64), calls=%async_computation.3 | async-start | bytes 393216 | tf_op jit(solution)/shard_map/all_to_all | solution.py:108
  36.1 5.8 %copy-start.6 = (bf16[256,6,64]{0,2,1:T(8,128)(2,1)}, bf16[256,6,64]{0,2,1:T(8,128)(2,1)S(1)}, u32[]{:S(2)}) copy-start(bf16[256,6,64]{0,2,1:T(8,128)(2,1)S(1)} %reshape.144) | copy-start | bytes 589828
  41.9 1.8 %copy-start.12 = (bf16[256,6,64]{0,2,1:T(8,128)(2,1)S(1)}, bf16[256,6,64]{0,2,1:T(8,128)(2,1)}, u32[]{:S(2)}) copy-start(bf16[256,6,64]{0,2,1:T(8,128)(2,1)} %reshape.146) | copy-start | bytes 589828
  41.9 1.8 %copy-start.13 = (bf16[256,6,64]{0,2,1:T(8,128)(2,1)S(1)}, bf16[256,6,64]{0,2,1:T(8,128)(2,1)}, u32[]{:S(2)}) copy-start(bf16[256,6,64]{0,2,1:T(8,128)(2,1)} %reshape.147) | copy-start | bytes 589828
  43.8 2.0 %copy-start.5 = (f32[6,256,256]{1,2,0:T(8,128)S(1)}, f32[6,256,256]{1,2,0:T(8,128)}, u32[]{:S(2)}) copy-start(f32[6,256,256]{1,2,0:T(8,128)} %get-tuple-element.24) | copy-start | bytes 4718596
  46.0 0.9 copy-start.1
  47.2 5.6 %copy-start.11 = (f32[64,2]{1,0:T(8,128)S(1)}, f32[64,2]{1,0:T(8,128)}, u32[]{:S(2)}) copy-start(f32[64,2]{1,0:T(8,128)} %broadcast_multiply_fusion) | copy-start | bytes 1540
  48.3 10.8 %all-to-all-start.4 = ((bf16[4,64,384]{2,1,0:T(8,128)(2,1)}), bf16[4,64,384]{2,1,0:T(8,128)(2,1)}, u32[]{:S(2)}, u32[]{:S(2)}) async-start(bf16[4,64,384]{2,1,0:T(8,128)(2,1)} %copy.67), calls=%async_computation.4 | async-start | bytes 393216 | tf_op jit(solution)/shard_map/all_to_all | solution.py:122
  59.1 9.7 %all-to-all-start.5 = ((bf16[4,64,384]{2,1,0:T(8,128)(2,1)}), bf16[4,64,384]{2,1,0:T(8,128)(2,1)}, u32[]{:S(2)}, u32[]{:S(2)}) async-start(bf16[4,64,384]{2,1,0:T(8,128)(2,1)} %copy.70), calls=%async_computation.5 | async-start | bytes 393216 | tf_op jit(solution)/shard_map/all_to_all | solution.py:123
  66.2 8.0 %copy-start.14 = (bf16[1,1536]{1,0:T(2,128)(2,1)S(1)}, bf16[1,1536]{1,0:T(2,128)(2,1)}, u32[]{:S(2)}) copy-start(bf16[1,1536]{1,0:T(2,128)(2,1)} %param.16) | copy-start | bytes 9220
  68.8 9.2 %all-to-all-start.6 = ((bf16[4,64,384]{2,1,0:T(8,128)(2,1)}), bf16[4,64,384]{2,1,0:T(8,128)(2,1)S(1)}, u32[]{:S(2)}, u32[]{:S(2)}) async-start(bf16[4,64,384]{2,1,0:T(8,128)(2,1)} %copy.73), calls=%async_computation.6 | async-start | bytes 393216 | tf_op jit(solution)/shard_map/all_to_all | solution.py:124
  74.2 4.1 %copy-start.16 = (f32[128]{0:T(128)S(1)}, f32[128]{0:T(128)}, u32[]{:S(2)}) copy-start(f32[128]{0:T(128)} %rsqrt.12) | copy-start | bytes 1540
  78.3 5.8 %copy-start.4 = (bf16[128,1536]{1,0:T(8,128)(2,1)S(1)}, bf16[128,1536]{1,0:T(8,128)(2,1)}, u32[]{:S(2)}) copy-start(bf16[128,1536]{1,0:T(8,128)(2,1)} %copy-done.3) | copy-start | bytes 1179652
  78.3 5.8 %copy-start.15 = (f32[128]{0:T(128)S(1)}, f32[128]{0:T(128)}, u32[]{:S(2)}) copy-start(f32[128]{0:T(128)} %div.42) | copy-start | bytes 1540
  84.5 14.4 %collective-permute-start = (bf16[128,1536]{1,0:T(8,128)(2,1)S(1)}, bf16[128,1536]{1,0:T(8,128)(2,1)S(1)}, u32[]{:S(2)}, u32[]{:S(2)}) collective-permute-start(bf16[128,1536]{1,0:T(8,128)(2,1)S(1)} %add_convert_fusion), channel_id=1, source_target_pairs={{4,0},{8,4},{12,8},{16,12},{20,16},{24,20},{28,24},{0,28},{5,1},{9... | collective-permute-start | bytes 1179656 | tf_op jit(solution)/shard_map/ppermute | solution.py:13
where the time goes:
time: 101 us; the launch traced here: 99.9 us
  starting transfers between devices  38.1 us (38%)
  local copies, waits for them, and re-layouts  25.1 us (25%)
  waiting for transfers between devices  17.1 us (17%)
  matrix products  15.4 us (15%)
  other arithmetic  3.9 us (4%)
    ppermute x1, starting transfers between devices, passed_along(): return lax.ppermute(block, axis, route)  7.88 us
    ppermute x1, waiting for transfers between devices, passed_along(): return lax.ppermute(block, axis, route)  6.56 us
    dot_general x1, matrix products, per_device(): lax.dot_general(joined, qkv_weight[0], (((1,), (1,)), ((), ())), preferre...  5.77 us
    all_to_all x1, starting transfers between devices, per_device(): lax.all_to_all(query_cols, 'seq', split_axis=1, concat_axis=0, tiled=True)  5.42 us
    all_to_all x1, waiting for transfers between devices, per_device(): lax.all_to_all(grad_cols, 'seq', split_axis=1, concat_axis=0, tiled=True)  4.89 us
    all_to_all x1, starting transfers between devices, per_device(): lax.all_to_all(grad_key, 'seq', split_axis=0, concat_axis=1, tiled=True)  4.53 us
    all_to_all x1, starting transfers between devices, per_device(): lax.all_to_all(grad_query, 'seq', split_axis=0, concat_axis=1, tiled=True)  4.48 us
    all_to_all x1, starting transfers between devices, per_device(): lax.all_to_all(key_cols, 'seq', split_axis=1, concat_axis=0, tiled=True)  4.4 us
  transfers between devices with their start and end apart: 8, of which 5 were waited for; matrix products, arithmetic and copies ran while one was open for 22% of the time, Pallas kernels for 0%

commit v1 on v0

--- a/solution.py
+++ b/solution.py
@@ -1,6 +1,10 @@
+import functools
+
 import jax
 import jax.numpy as jnp
 from jax import lax
+from jax.experimental import pallas as pl
+from jax.experimental.pallas import tpu as pltpu
 from jax.sharding import PartitionSpec as P
 
 HEADS_W = 12
@@ -141,6 +145,274 @@
     return passed.reshape(1, frames, record_count, feature_count)
 
 
+UNIT = 2 * HD
+NT = (((1,), (1,)), ((), ()))
+TN = (((0,), (0,)), ((), ()))
+NN = (((1,), (0,)), ((), ()))
+
+
+def mm(lhs, rhs, dims):
+    return lax.dot_general(lhs, rhs, dims, preferred_element_type=jnp.float32)
+
+
+def unit_attention(q, k, v, g, key_length):
+    length = q.shape[0]
+    first = lax.broadcasted_iota(jnp.int32, (1, UNIT), 1) < HD
+    usable = lax.broadcasted_iota(jnp.int32, (length, 1), 0) < key_length
+    zero = jnp.zeros((), k.dtype)
+    halves = []
+    for head in range(2):
+        k_head = jnp.where(first, k, zero) if head == 0 else jnp.where(first, zero, k)
+        v_head = jnp.where(first, v, zero) if head == 0 else jnp.where(first, zero, v)
+        scores = jnp.where(usable, mm(k_head, q, NT), -jnp.inf)
+        terms = jnp.exp(scores - jnp.max(scores, axis=0, keepdims=True))
+        prob = terms * (1.0 / jnp.sum(terms, axis=0, keepdims=True))
+        grad_prob = mm(v_head, g, NT)
+        delta = jnp.sum(prob * grad_prob, axis=0, keepdims=True)
+        grad_score = (prob * (grad_prob - delta)).astype(jnp.bfloat16)
+        halves.append((
+            mm(grad_score, k, TN) * (HD ** -0.5),
+            mm(grad_score, q, NN),
+            mm(prob.astype(jnp.bfloat16), g, NN),
+        ))
+    return [jnp.where(first, a, b).astype(jnp.bfloat16) for a, b in zip(*halves)]
+
+
+def fused_kernel(
+    n, pipes, frames, recs, width, inner,
+    lens, gain, q_h, k_h, v_h, go_h, ow_h, li_h, qw_h,
+    out,
+    q_v, k_v, v_v, go_v, ow_v, li_v, qw_v, g32, st, stg, rx, rxg, rs, jn, acc, normed, inv,
+    o_send, o_recv, o32,
+    load_sem, fs, fr, gs, gr, bs, br, ps, pr,
+):
+    seq, pipe = lax.axis_index("seq"), lax.axis_index("pipe")
+    per_rec = inner // UNIT
+    units = recs * per_rec
+    phases = units // n
+    length = n * frames
+
+    loads = [
+        pltpu.make_async_copy(src, dst, load_sem.at[i])
+        for i, (src, dst) in enumerate(
+            [(q_h, q_v), (k_h, k_v), (v_h, v_v), (go_h, go_v), (ow_h, ow_v), (li_h, li_v), (qw_h, qw_v)]
+        )
+    ]
+    for load in loads:
+        load.start()
+
+    peers = [lax.rem(seq + off, n) for off in range(1, n)]
+    before, after = lax.rem(pipe + pipes - 1, pipes), lax.rem(pipe + 1, pipes)
+    barrier = pltpu.get_barrier_semaphore()
+    for peer in peers:
+        pl.semaphore_signal(barrier, inc=1, device_id=(pipe, peer), device_id_type=pl.DeviceIdType.MESH)
+    for other in (before, after):
+        pl.semaphore_signal(barrier, inc=1, device_id=(other, seq), device_id_type=pl.DeviceIdType.MESH)
+
+    def send(src, dst, s_sem, r_sem, to):
+        return pltpu.make_async_remote_copy(
+            src_ref=src, dst_ref=dst, send_sem=s_sem, recv_sem=r_sem,
+            device_id=to, device_id_type=pl.DeviceIdType.MESH,
+        )
+
+    def forward(p):
+        return [
+            send(st.at[p * n + d], rx.at[p, pl.ds(0, 3), seq], fs.at[p, i], fr.at[p, i], (pipe, d))
+            for i, d in enumerate(peers)
+        ]
+
+    def forward_grad(p):
+        return [
+            send(stg.at[p * n + d], rxg.at[p, seq], gs.at[p, i], gr.at[p, i], (pipe, d))
+            for i, d in enumerate(peers)
+        ]
+
+    def back(p):
+        return [
+            send(rs.at[p, d], jn.at[p * n + seq], bs.at[p, i], br.at[p, i], (pipe, d))
+            for i, d in enumerate(peers)
+        ]
+
+    def along(r):
+        return send(o_send.at[r], o_recv.at[r], ps.at[r], pr.at[r], (before, seq))
+
+    def start(copies):
+        for copy in copies:
+            copy.start()
+
+    for load in loads[:3]:
+        load.wait()
+    for t, src in enumerate((q_v, k_v, v_v)):
+        for r in range(recs):
+            rows = src[:, r, :]
+            if t == 0:
+                rows = rows * jnp.asarray(HD ** -0.5, rows.dtype)
+            for j in range(per_rec):
+                st[r * per_rec + j, t] = rows[:, j * UNIT : (j + 1) * UNIT]
+    pl.semaphore_wait(barrier, n + 1)
+    start(forward(0))
+
+    loads[3].wait()
+    loads[4].wait()
+    product = mm(go_v[...].reshape(frames * recs, width), ow_v[...], NT)
+    for j in range(per_rec):
+        g32[j] = product[:, j * UNIT : (j + 1) * UNIT]
+    for r in range(recs):
+        for j in range(per_rec):
+            rows = g32[j, pl.ds(r, frames, stride=recs), :]
+            stg[r * per_rec + j] = rows.astype(jnp.bfloat16)
+    start(forward_grad(0))
+    for p in range(1, phases):
+        start(forward(p))
+        start(forward_grad(p))
+
+    for p in range(phases):
+        for t in range(3):
+            rx[p, t, seq] = st[p * n + seq, t]
+        rxg[p, seq] = stg[p * n + seq]
+
+    loads[5].wait()
+    for r in range(recs):
+        inputs = li_v[:, r, :].astype(jnp.float32)
+        centred = inputs - jnp.mean(inputs, axis=-1, keepdims=True)
+        inv_std = lax.rsqrt(jnp.mean(centred * centred, axis=-1, keepdims=True) + 1e-05)
+        normed[r] = centred * inv_std
+        inv[r] = jnp.broadcast_to(inv_std, (frames, 128))
+
+    def attention(p):
+        for copy in forward(p) + forward_grad(p):
+            copy.wait_recv()
+        q, k, v = (rx[p, t].reshape(length, UNIT) for t in range(3))
+        g = rxg[p].reshape(length, UNIT)
+        rec = lax.div(p * n + seq, per_rec)
+        key_length = lens[0]
+        for r in range(1, recs):
+            key_length = jnp.where(rec == r, lens[r], key_length)
+        for t, grad in enumerate(unit_attention(q, k, v, g, key_length)):
+            rs[p, :, t] = grad.reshape(n, frames, UNIT)
+        start(back(p))
+        for t in range(3):
+            jn[p * n + seq, t] = rs[p, seq, t]
+
+    def project(p):
+        for copy in back(p):
+            copy.wait_recv()
+        for r in range(recs):
+            low, high = max(p * n, r * per_rec), min((p + 1) * n, (r + 1) * per_rec)
+            if low >= high:
+                continue
+            for t in range(3):
+                block = jnp.concatenate([jn[u, t] for u in range(low, high)], axis=1)
+                column = t * inner + (low - r * per_rec) * UNIT
+                part = mm(block, qw_v[:, column : column + (high - low) * UNIT], NT)
+                if low == r * per_rec and t == 0:
+                    acc[r] = part
+                else:
+                    acc[r] += part
+            if high == (r + 1) * per_rec:
+                scaled = acc[r] * gain[...].astype(jnp.float32)
+                rows = normed[r]
+                branch = inv[r][:, :1] * (
+                    scaled
+                    - jnp.mean(scaled, axis=-1, keepdims=True)
+                    - rows * jnp.mean(scaled * rows, axis=-1, keepdims=True)
+                )
+                o_send[r] = (go_v[:, r, :].astype(jnp.float32) + branch).astype(jnp.bfloat16)
+                along(r).start()
+
+    for p in range(phases):
+        attention(p)
+        if p == 1:
+            loads[6].wait()
+        if p >= 1:
+            project(p - 1)
+    if phases == 1:
+        loads[6].wait()
+    project(phases - 1)
+    for r in range(recs):
+        along(r).wait_recv()
+        o32[:, r, :] = o_recv[r].astype(jnp.float32)
+    out[...] = o32[...].astype(jnp.bfloat16)
+    for p in range(phases):
+        for copy in forward(p) + forward_grad(p) + back(p):
+            copy.wait_send()
+    for r in range(recs):
+        along(r).wait_send()
+
+
+def per_device_fused(
+    layer_input, grad_out, queries, keys_saved, values_saved, out_weight, qkv_weight, ln_gain, lengths
+):
+    n, pipes = lax.axis_size("seq"), lax.axis_size("pipe")
+    _, frames, recs, width = grad_out.shape
+    inner = out_weight.shape[1]
+    per_rec = inner // UNIT
+    units = recs * per_rec
+    phases = units // n
+    bf16, f32 = jnp.bfloat16, jnp.float32
+    vmem, hbm = pl.BlockSpec(memory_space=pltpu.VMEM), pl.BlockSpec(memory_space=pl.ANY)
+    pairs = pltpu.SemaphoreType.DMA((phases, n - 1))
+    scratch = [
+        pltpu.VMEM((frames, recs, inner), bf16),
+        pltpu.VMEM((frames, recs, inner), bf16),
+        pltpu.VMEM((frames, recs, inner), bf16),
+        pltpu.VMEM((frames, recs, width), bf16),
+        pltpu.VMEM((inner, width), bf16),
+        pltpu.VMEM((frames, recs, width), bf16),
+        pltpu.VMEM((width, 3 * inner), bf16),
+        pltpu.VMEM((per_rec, frames * recs, UNIT), f32),
+        pltpu.VMEM((units, 3, frames, UNIT), bf16),
+        pltpu.VMEM((units, frames, UNIT), bf16),
+        pltpu.VMEM((phases, 3, n, frames, UNIT), bf16),
+        pltpu.VMEM((phases, n, frames, UNIT), bf16),
+        pltpu.VMEM((phases, n, 3, frames, UNIT), bf16),
+        pltpu.VMEM((units, 3, frames, UNIT), bf16),
+        pltpu.VMEM((recs, frames, width), f32),
+        pltpu.VMEM((recs, frames, width), f32),
+        pltpu.VMEM((recs, frames, 128), f32),
+        pltpu.VMEM((recs, frames, width), bf16),
+        pltpu.VMEM((recs, frames, width), bf16),
+        pltpu.VMEM((frames, recs, width), f32),
+        pltpu.SemaphoreType.DMA((7,)),
+        pairs, pairs, pairs, pairs, pairs, pairs,
+        pltpu.SemaphoreType.DMA((recs,)),
+        pltpu.SemaphoreType.DMA((recs,)),
+    ]
+    passed = pl.pallas_call(
+        functools.partial(fused_kernel, n, pipes, frames, recs, width, inner),
+        out_shape=jax.ShapeDtypeStruct((frames, recs, width), bf16),
+        in_specs=[pl.BlockSpec(memory_space=pltpu.SMEM), vmem] + [hbm] * 7,
+        out_specs=vmem,
+        scratch_shapes=scratch,
+        compiler_params=pltpu.CompilerParams(
+            collective_id=0, has_side_effects=True, vmem_limit_bytes=40 * 1024 * 1024
+        ),
+        cost_estimate=pl.CostEstimate(
+            flops=8 * frames * recs * width * inner, bytes_accessed=8 * width * inner, transcendentals=0
+        ),
+    )(
+        lengths[0], ln_gain, queries[0], keys_saved[0], values_saved[0], grad_out[0], out_weight[0],
+        layer_input[0], qkv_weight[0],
+    )
+    return passed[None]
+
+
+def body_for(
+    layer_input, grad_out, queries, keys_saved, values_saved, out_weight, qkv_weight, ln_gain, lengths
+):
+    args = (
+        layer_input, grad_out, queries, keys_saved, values_saved, out_weight, qkv_weight, ln_gain, lengths
+    )
+    n, pipes = lax.axis_size("seq"), lax.axis_size("pipe")
+    _, frames, recs, _ = grad_out.shape
+    inner = out_weight.shape[1]
+    fits = (
+        inner % UNIT == 0 and (recs * (inner // UNIT)) % n == 0 and n > 1 and pipes > 2
+        and frames % 16 == 0 and n * frames <= 256 and recs == 2
+    )
+    return per_device_fused(*args) if fits else per_device(*args)
+
+
 def solution(mesh):
     placed = (
         P("pipe", "seq", None, None),
@@ -154,7 +426,7 @@
         P("pipe", None),
     )
     return jax.shard_map(
-        per_device,
+        body_for,
         mesh=mesh,
         in_specs=placed,
         out_specs=P("pipe", "seq", None, None),

time: 101 us -> 58.8 us (0.58)
  Pallas kernels: 0 us -> 46.9 us
  starting transfers between devices: 38.1 us -> 0 us
  waiting for transfers between devices: 17.1 us -> 0 us
  matrix products: 15.4 us -> 0 us
  local copies, waits for them, and re-layouts: 25.1 us -> 11.5 us
  other arithmetic: 3.9 us -> 0 us
    pallas_call x0 -> x1, Pallas kernels: none -> 46.9 us  [per_device_fused(): pl.pallas_call(functools.partial(fused_kernel, n, pipes, frames, recs, wi...]
    all_to_all x7 -> x0, starting transfers between devices: 30.2 us -> none  [the longest x1 5.42 us: per_device(): lax.all_to_all(query_cols, 'seq', split_axis=1, concat_axis=0, tiled=True)]
    all_to_all x21 -> x0, local copies, waits for them, and re-layouts: 17.5 us -> none  [the longest x3 3.16 us: per_device(): lax.all_to_all(grad_key, 'seq', split_axis=0, concat_axis=1, tiled=True)]
    dot_general x6 -> x0, matrix products: 13.6 us -> none  [the longest x1 5.77 us: per_device(): lax.dot_general(joined, qkv_weight[0], (((1,), (1,)), ((), ())), preferre...]
    unnamed x36 -> x19, local copies, waits for them, and re-layouts: 0.94 us -> 11.5 us
    all_to_all x7 -> x0, waiting for transfers between devices: 10.5 us -> none  [the longest x1 4.89 us: per_device(): lax.all_to_all(grad_cols, 'seq', split_axis=1, concat_axis=0, tiled=True)]
    ppermute x1 -> x0, starting transfers between devices: 7.88 us -> none  [passed_along(): return lax.ppermute(block, axis, route)]
    ppermute x1 -> x0, waiting for transfers between devices: 6.56 us -> none  [passed_along(): return lax.ppermute(block, axis, route)]
  transfers between devices with their start and end apart: 8 -> 0, of which waited for: 5 -> 0; matrix products, arithmetic and copies ran while one was open for 22% -> 0% of each run, Pallas kernels for 0% -> 0%
where the time goes in v1:
time: 58.8 us; the launch traced here: 58.4 us
  Pallas kernels  46.9 us (80%)
  local copies, waits for them, and re-layouts  11.5 us (20%)
    pallas_call x1, Pallas kernels, per_device_fused(): pl.pallas_call(functools.partial(fused_kernel, n, pipes, frames, recs, wi...  46.9 us
    unnamed x19, local copies, waits for them, and re-layouts  11.5 us

profile of v1, /device:TPU:1, one launch (start us, length us, event | category | flops | bytes accessed | tf_op | source)
XLA Modules:
  0.0 58.4 jit_solution(15235802151612033317)
XLA Ops:
  0.0 0.0 copy-start
  0.0 3.0 %copy-done = bf16[1,1536,2304]{2,1,0:T(8,128)(2,1)S(1)} copy-done((bf16[1,1536,2304]{2,1,0:T(8,128)(2,1)S(1)}, bf16[1,1536,2304]{2,1,0:T(8,128)(2,1)}, u32[]{:S(2)}) %copy-start) | copy-done | bytes 7077912
  3.0 0.0 copy-start.1
  3.0 1.7 %copy-done.1 = bf16[1,768,1536]{2,1,0:T(8,128)(2,1)S(1)} copy-done((bf16[1,768,1536]{2,1,0:T(8,128)(2,1)S(1)}, bf16[1,768,1536]{2,1,0:T(8,128)(2,1)}, u32[]{:S(2)}) %copy-start.1) | copy-done | bytes 2359320
  4.7 0.0 copy-start.2
  4.7 1.0 %copy-done.2 = bf16[1,64,2,1536]{3,2,1,0:T(2,128)(2,1)S(1)} copy-done((bf16[1,64,2,1536]{3,2,1,0:T(2,128)(2,1)S(1)}, bf16[1,64,2,1536]{3,2,1,0:T(2,128)(2,1)}, u32[]{:S(2)}) %copy-start.2) | copy-done | bytes 393240
  5.7 0.0 copy-start.3
  5.7 1.0 %copy-done.3 = bf16[1,64,2,1536]{3,2,1,0:T(2,128)(2,1)S(1)} copy-done((bf16[1,64,2,1536]{3,2,1,0:T(2,128)(2,1)S(1)}, bf16[1,64,2,1536]{3,2,1,0:T(2,128)(2,1)}, u32[]{:S(2)}) %copy-start.3) | copy-done | bytes 393240
  6.7 0.0 copy-start.4
  6.7 0.9 %copy-done.4 = bf16[1,64,2,768]{3,2,1,0:T(2,128)(2,1)S(1)} copy-done((bf16[1,64,2,768]{3,2,1,0:T(2,128)(2,1)S(1)}, bf16[1,64,2,768]{3,2,1,0:T(2,128)(2,1)}, u32[]{:S(2)}) %copy-start.4) | copy-done | bytes 196632
  7.6 0.0 copy-start.5
  7.6 0.9 %copy-done.5 = bf16[1,64,2,768]{3,2,1,0:T(2,128)(2,1)S(1)} copy-done((bf16[1,64,2,768]{3,2,1,0:T(2,128)(2,1)S(1)}, bf16[1,64,2,768]{3,2,1,0:T(2,128)(2,1)}, u32[]{:S(2)}) %copy-start.5) | copy-done | bytes 196632
  8.5 0.0 copy-start.6
  8.5 0.9 %copy-done.6 = bf16[1,64,2,768]{3,2,1,0:T(2,128)(2,1)S(1)} copy-done((bf16[1,64,2,768]{3,2,1,0:T(2,128)(2,1)S(1)}, bf16[1,64,2,768]{3,2,1,0:T(2,128)(2,1)}, u32[]{:S(2)}) %copy-start.6) | copy-done | bytes 196632
  9.4 0.0 copy-start.7
  9.5 0.7 %copy-done.7 = bf16[1,1536]{1,0:T(2,128)(2,1)S(1)} copy-done((bf16[1,1536]{1,0:T(2,128)(2,1)S(1)}, bf16[1,1536]{1,0:T(2,128)(2,1)}, u32[]{:S(2)}) %copy-start.7) | copy-done | bytes 3096
  10.1 0.0 copy-start.8
  10.1 0.7 %copy-done.8 = s32[1,2]{1,0:T(1,128)S(1)} copy-done((s32[1,2]{1,0:T(1,128)S(1)}, s32[1,2]{1,0:T(1,128)}, u32[]{:S(2)}) %copy-start.8) | copy-done | bytes 32
  10.8 46.9 %shard_map.91 = bf16[64,2,1536]{2,1,0:T(2,128)(2,1)S(1)} custom-call(s32[2]{0:T(128)S(1)} %bitcast.17, bf16[1,1536]{1,0:T(2,128)(2,1)S(1)} %copy-done.7, bf16[64,2,768]{2,1,0:T(2,128)(2,1)S(1)} %bitcast.14, bf16[64,2,768]{2,1,0:T(2,128)(2,1)S(1)} %bitcast.15, bf16[64,2,768]{2,1,0:T(2,128)(2,1)S(1)} %bitcast.16, bf16[64,2,1536]{2,1,0:T(2,128)(2,1)S(1)} %bitcast.12, ...), custom_call_target="tpu_custom_call" | custom-call | flops 1207959552 | bytes 9437184 | tf_op jit(solution)/shard_map/pallas_call | solution.py:381
  57.7 0.7 %copy.11 = bf16[1,64,2,1536]{3,2,1,0:T(2,128)(2,1)} copy(bf16[1,64,2,1536]{3,2,1,0:T(2,128)(2,1)S(1)} %bitcast.11) | data formatting | bytes 786432
Async XLA Ops:
  0.0 3.0 %copy-start = (bf16[1,1536,2304]{2,1,0:T(8,128)(2,1)S(1)}, bf16[1,1536,2304]{2,1,0:T(8,128)(2,1)}, u32[]{:S(2)}) copy-start(bf16[1,1536,2304]{2,1,0:T(8,128)(2,1)} %param.15) | copy-start | bytes 21233668
  3.0 1.7 %copy-start.1 = (bf16[1,768,1536]{2,1,0:T(8,128)(2,1)S(1)}, bf16[1,768,1536]{2,1,0:T(8,128)(2,1)}, u32[]{:S(2)}) copy-start(bf16[1,768,1536]{2,1,0:T(8,128)(2,1)} %param.14) | copy-start | bytes 7077892
  4.7 1.0 %copy-start.2 = (bf16[1,64,2,1536]{3,2,1,0:T(2,128)(2,1)S(1)}, bf16[1,64,2,1536]{3,2,1,0:T(2,128)(2,1)}, u32[]{:S(2)}) copy-start(bf16[1,64,2,1536]{3,2,1,0:T(2,128)(2,1)} %param.10) | copy-start | bytes 1179652
  5.7 1.0 %copy-start.3 = (bf16[1,64,2,1536]{3,2,1,0:T(2,128)(2,1)S(1)}, bf16[1,64,2,1536]{3,2,1,0:T(2,128)(2,1)}, u32[]{:S(2)}) copy-start(bf16[1,64,2,1536]{3,2,1,0:T(2,128)(2,1)} %param.9) | copy-start | bytes 1179652
  6.7 0.9 %copy-start.4 = (bf16[1,64,2,768]{3,2,1,0:T(2,128)(2,1)S(1)}, bf16[1,64,2,768]{3,2,1,0:T(2,128)(2,1)}, u32[]{:S(2)}) copy-start(bf16[1,64,2,768]{3,2,1,0:T(2,128)(2,1)} %param.11) | copy-start | bytes 589828
  7.6 0.9 %copy-start.5 = (bf16[1,64,2,768]{3,2,1,0:T(2,128)(2,1)S(1)}, bf16[1,64,2,768]{3,2,1,0:T(2,128)(2,1)}, u32[]{:S(2)}) copy-start(bf16[1,64,2,768]{3,2,1,0:T(2,128)(2,1)} %param.12) | copy-start | bytes 589828
  8.5 0.9 %copy-start.6 = (bf16[1,64,2,768]{3,2,1,0:T(2,128)(2,1)S(1)}, bf16[1,64,2,768]{3,2,1,0:T(2,128)(2,1)}, u32[]{:S(2)}) copy-start(bf16[1,64,2,768]{3,2,1,0:T(2,128)(2,1)} %param.13) | copy-start | bytes 589828
  9.4 0.7 %copy-start.7 = (bf16[1,1536]{1,0:T(2,128)(2,1)S(1)}, bf16[1,1536]{1,0:T(2,128)(2,1)}, u32[]{:S(2)}) copy-start(bf16[1,1536]{1,0:T(2,128)(2,1)} %gain.1) | copy-start | bytes 9220
  10.1 0.7 %copy-start.8 = (s32[1,2]{1,0:T(1,128)S(1)}, s32[1,2]{1,0:T(1,128)}, u32[]{:S(2)}) copy-start(s32[1,2]{1,0:T(1,128)} %param.17) | copy-start | bytes 28

commit v2 on v1

--- a/solution.py
+++ b/solution.py
@@ -242,15 +242,17 @@
 
     for load in loads[:3]:
         load.wait()
-    for t, src in enumerate((q_v, k_v, v_v)):
-        for r in range(recs):
+    for r in range(recs):
+        for t, src in enumerate((q_v, k_v, v_v)):
             rows = src[:, r, :]
             if t == 0:
                 rows = rows * jnp.asarray(HD ** -0.5, rows.dtype)
             for j in range(per_rec):
                 st[r * per_rec + j, t] = rows[:, j * UNIT : (j + 1) * UNIT]
-    pl.semaphore_wait(barrier, n + 1)
-    start(forward(0))
+        if r == 0:
+            pl.semaphore_wait(barrier, n + 1)
+        if n <= (r + 1) * per_rec < n + per_rec:
+            start(forward(0))
 
     loads[3].wait()
     loads[4].wait()
@@ -262,9 +264,9 @@
             rows = g32[j, pl.ds(r, frames, stride=recs), :]
             stg[r * per_rec + j] = rows.astype(jnp.bfloat16)
     start(forward_grad(0))
-    for p in range(1, phases):
-        start(forward(p))
-        start(forward_grad(p))
+    if phases > 1:
+        start(forward(1))
+        start(forward_grad(1))
 
     for p in range(phases):
         for t in range(3):
@@ -282,6 +284,9 @@
     def attention(p):
         for copy in forward(p) + forward_grad(p):
             copy.wait_recv()
+        if p + 2 < phases:
+            start(forward(p + 2))
+            start(forward_grad(p + 2))
         q, k, v = (rx[p, t].reshape(length, UNIT) for t in range(3))
         g = rxg[p].reshape(length, UNIT)
         rec = lax.div(p * n + seq, per_rec)
@@ -350,7 +355,7 @@
     units = recs * per_rec
     phases = units // n
     bf16, f32 = jnp.bfloat16, jnp.float32
-    vmem, hbm = pl.BlockSpec(memory_space=pltpu.VMEM), pl.BlockSpec(memory_space=pl.ANY)
+    vmem, hbm = pl.BlockSpec(memory_space=pltpu.VMEM), pl.BlockSpec(memory_space=pltpu.HBM)
     pairs = pltpu.SemaphoreType.DMA((phases, n - 1))
     scratch = [
         pltpu.VMEM((frames, recs, inner), bf16),
@@ -385,7 +390,7 @@
         out_specs=vmem,
         scratch_shapes=scratch,
         compiler_params=pltpu.CompilerParams(
-            collective_id=0, has_side_effects=True, vmem_limit_bytes=40 * 1024 * 1024
+            collective_id=0, has_side_effects=True, vmem_limit_bytes=52 * 1024 * 1024
         ),
         cost_estimate=pl.CostEstimate(
             flops=8 * frames * recs * width * inner, bytes_accessed=8 * width * inner, transcendentals=0

time: 58.8 us -> 53.1 us (0.903)
  local copies, waits for them, and re-layouts: 11.5 us -> 6.86 us
  Pallas kernels: 46.9 us -> 45.9 us
    unnamed x19 -> x15, local copies, waits for them, and re-layouts: 11.5 us -> 6.86 us
    pallas_call x1, Pallas kernels: 46.9 us -> 45.9 us  [per_device_fused(): pl.pallas_call(functools.partial(fused_kernel, n, pipes, frames, recs, wi...]
where the time goes in v2:
time: 53.1 us; the launch traced here: 52.7 us
  Pallas kernels  45.9 us (86%)
  local copies, waits for them, and re-layouts  6.86 us (13%)
    pallas_call x1, Pallas kernels, per_device_fused(): pl.pallas_call(functools.partial(fused_kernel, n, pipes, frames, recs, wi...  45.9 us
    unnamed x15, local copies, waits for them, and re-layouts  6.86 us

profile of v2, /device:TPU:1, one launch (start us, length us, event | category | flops | bytes accessed | tf_op | source)
XLA Modules:
  0.0 52.7 jit_solution(13113775104185603057)
XLA Ops:
  0.0 0.0 copy-start
  0.0 1.0 %copy-done = bf16[1,64,2,1536]{3,2,1,0:T(2,128)(2,1)S(1)} copy-done((bf16[1,64,2,1536]{3,2,1,0:T(2,128)(2,1)S(1)}, bf16[1,64,2,1536]{3,2,1,0:T(2,128)(2,1)}, u32[]{:S(2)}) %copy-start) | copy-done | bytes 393240
  1.0 0.0 copy-start.1
  1.0 1.0 %copy-done.1 = bf16[1,64,2,1536]{3,2,1,0:T(2,128)(2,1)S(1)} copy-done((bf16[1,64,2,1536]{3,2,1,0:T(2,128)(2,1)S(1)}, bf16[1,64,2,1536]{3,2,1,0:T(2,128)(2,1)}, u32[]{:S(2)}) %copy-start.1) | copy-done | bytes 393240
  2.0 0.0 copy-start.2
  2.0 0.9 %copy-done.2 = bf16[1,64,2,768]{3,2,1,0:T(2,128)(2,1)S(1)} copy-done((bf16[1,64,2,768]{3,2,1,0:T(2,128)(2,1)S(1)}, bf16[1,64,2,768]{3,2,1,0:T(2,128)(2,1)}, u32[]{:S(2)}) %copy-start.2) | copy-done | bytes 196632
  2.9 0.0 copy-start.3
  2.9 0.9 %copy-done.3 = bf16[1,64,2,768]{3,2,1,0:T(2,128)(2,1)S(1)} copy-done((bf16[1,64,2,768]{3,2,1,0:T(2,128)(2,1)S(1)}, bf16[1,64,2,768]{3,2,1,0:T(2,128)(2,1)}, u32[]{:S(2)}) %copy-start.3) | copy-done | bytes 196632
  3.8 0.0 copy-start.4
  3.9 0.9 %copy-done.4 = bf16[1,64,2,768]{3,2,1,0:T(2,128)(2,1)S(1)} copy-done((bf16[1,64,2,768]{3,2,1,0:T(2,128)(2,1)S(1)}, bf16[1,64,2,768]{3,2,1,0:T(2,128)(2,1)}, u32[]{:S(2)}) %copy-start.4) | copy-done | bytes 196632
  4.8 0.0 copy-start.5
  4.8 0.7 %copy-done.5 = bf16[1,1536]{1,0:T(2,128)(2,1)S(1)} copy-done((bf16[1,1536]{1,0:T(2,128)(2,1)S(1)}, bf16[1,1536]{1,0:T(2,128)(2,1)}, u32[]{:S(2)}) %copy-start.5) | copy-done | bytes 3096
  5.5 0.0 copy-start.6
  5.5 0.7 %copy-done.6 = s32[1,2]{1,0:T(1,128)S(1)} copy-done((s32[1,2]{1,0:T(1,128)S(1)}, s32[1,2]{1,0:T(1,128)}, u32[]{:S(2)}) %copy-start.6) | copy-done | bytes 32
  6.1 45.9 %shard_map.91 = bf16[64,2,1536]{2,1,0:T(2,128)(2,1)S(1)} custom-call(s32[2]{0:T(128)S(1)} %bitcast.15, bf16[1,1536]{1,0:T(2,128)(2,1)S(1)} %copy-done.5, bf16[64,2,768]{2,1,0:T(2,128)(2,1)S(1)} %bitcast.12, bf16[64,2,768]{2,1,0:T(2,128)(2,1)S(1)} %bitcast.13, bf16[64,2,768]{2,1,0:T(2,128)(2,1)S(1)} %bitcast.14, bf16[64,2,1536]{2,1,0:T(2,128)(2,1)S(1)} %bitcast.10, ...), custom_call_target="tpu_custom_call" | custom-call | flops 1207959552 | bytes 9437184 | tf_op jit(solution)/shard_map/pallas_call | solution.py:386
  52.0 0.7 %copy.11 = bf16[1,64,2,1536]{3,2,1,0:T(2,128)(2,1)} copy(bf16[1,64,2,1536]{3,2,1,0:T(2,128)(2,1)S(1)} %bitcast.9) | data formatting | bytes 786432
Async XLA Ops:
  0.0 1.0 %copy-start = (bf16[1,64,2,1536]{3,2,1,0:T(2,128)(2,1)S(1)}, bf16[1,64,2,1536]{3,2,1,0:T(2,128)(2,1)}, u32[]{:S(2)}) copy-start(bf16[1,64,2,1536]{3,2,1,0:T(2,128)(2,1)} %param.10) | copy-start | bytes 1179652
  1.0 1.0 %copy-start.1 = (bf16[1,64,2,1536]{3,2,1,0:T(2,128)(2,1)S(1)}, bf16[1,64,2,1536]{3,2,1,0:T(2,128)(2,1)}, u32[]{:S(2)}) copy-start(bf16[1,64,2,1536]{3,2,1,0:T(2,128)(2,1)} %param.9) | copy-start | bytes 1179652
  2.0 0.9 %copy-start.2 = (bf16[1,64,2,768]{3,2,1,0:T(2,128)(2,1)S(1)}, bf16[1,64,2,768]{3,2,1,0:T(2,128)(2,1)}, u32[]{:S(2)}) copy-start(bf16[1,64,2,768]{3,2,1,0:T(2,128)(2,1)} %param.11) | copy-start | bytes 589828
  2.9 0.9 %copy-start.3 = (bf16[1,64,2,768]{3,2,1,0:T(2,128)(2,1)S(1)}, bf16[1,64,2,768]{3,2,1,0:T(2,128)(2,1)}, u32[]{:S(2)}) copy-start(bf16[1,64,2,768]{3,2,1,0:T(2,128)(2,1)} %param.12) | copy-start | bytes 589828
  3.8 0.9 %copy-start.4 = (bf16[1,64,2,768]{3,2,1,0:T(2,128)(2,1)S(1)}, bf16[1,64,2,768]{3,2,1,0:T(2,128)(2,1)}, u32[]{:S(2)}) copy-start(bf16[1,64,2,768]{3,2,1,0:T(2,128)(2,1)} %param.13) | copy-start | bytes 589828
  4.8 0.7 %copy-start.5 = (bf16[1,1536]{1,0:T(2,128)(2,1)S(1)}, bf16[1,1536]{1,0:T(2,128)(2,1)}, u32[]{:S(2)}) copy-start(bf16[1,1536]{1,0:T(2,128)(2,1)} %gain.1) | copy-start | bytes 9220
  5.5 0.7 %copy-start.6 = (s32[1,2]{1,0:T(1,128)S(1)}, s32[1,2]{1,0:T(1,128)}, u32[]{:S(2)}) copy-start(s32[1,2]{1,0:T(1,128)} %param.17) | copy-start | bytes 28

commit v3 on v2

--- a/solution.py
+++ b/solution.py
@@ -227,14 +227,26 @@
             for i, d in enumerate(peers)
         ]
 
-    def back(p):
+    def pieces(p):
+        count = 2 if p == phases - 1 else 1
+        return [(i, pl.ds(i * (frames // count), frames // count)) for i in range(count)]
+
+    def whole_at(r):
+        return ((r + 1) * per_rec - 1) // n
+
+    def back(p, part, rows):
         return [
-            send(rs.at[p, d], jn.at[p * n + seq], bs.at[p, i], br.at[p, i], (pipe, d))
+            send(
+                rs.at[p, d, pl.ds(0, 3), rows], jn.at[p * n + seq, pl.ds(0, 3), rows],
+                bs.at[p, part, i], br.at[p, part, i], (pipe, d),
+            )
             for i, d in enumerate(peers)
         ]
 
-    def along(r):
-        return send(o_send.at[r], o_recv.at[r], ps.at[r], pr.at[r], (before, seq))
+    def along(r, part, rows):
+        return send(
+            o_send.at[r, rows], o_recv.at[r, rows], ps.at[r, part], pr.at[r, part], (before, seq)
+        )
 
     def start(copies):
         for copy in copies:
@@ -295,54 +307,58 @@
             key_length = jnp.where(rec == r, lens[r], key_length)
         for t, grad in enumerate(unit_attention(q, k, v, g, key_length)):
             rs[p, :, t] = grad.reshape(n, frames, UNIT)
-        start(back(p))
+        for part, rows in pieces(p):
+            start(back(p, part, rows))
         for t in range(3):
             jn[p * n + seq, t] = rs[p, seq, t]
 
-    def project(p):
-        for copy in back(p):
+    def project(p, part, rows):
+        for copy in back(p, part, rows):
             copy.wait_recv()
         for r in range(recs):
             low, high = max(p * n, r * per_rec), min((p + 1) * n, (r + 1) * per_rec)
             if low >= high:
                 continue
+            total = None if low == r * per_rec else acc[r, rows]
             for t in range(3):
-                block = jnp.concatenate([jn[u, t] for u in range(low, high)], axis=1)
+                block = jnp.concatenate([jn[u, t, rows] for u in range(low, high)], axis=1)
                 column = t * inner + (low - r * per_rec) * UNIT
-                part = mm(block, qw_v[:, column : column + (high - low) * UNIT], NT)
-                if low == r * per_rec and t == 0:
-                    acc[r] = part
-                else:
-                    acc[r] += part
-            if high == (r + 1) * per_rec:
-                scaled = acc[r] * gain[...].astype(jnp.float32)
-                rows = normed[r]
-                branch = inv[r][:, :1] * (
+                term = mm(block, qw_v[:, column : column + (high - low) * UNIT], NT)
+                total = term if total is None else total + term
+            if p < whole_at(r):
+                acc[r, rows] = total
+            else:
+                scaled = total * gain[...].astype(jnp.float32)
+                unit = normed[r, rows]
+                branch = inv[r, rows][:, :1] * (
                     scaled
                     - jnp.mean(scaled, axis=-1, keepdims=True)
-                    - rows * jnp.mean(scaled * rows, axis=-1, keepdims=True)
+                    - unit * jnp.mean(scaled * unit, axis=-1, keepdims=True)
                 )
-                o_send[r] = (go_v[:, r, :].astype(jnp.float32) + branch).astype(jnp.bfloat16)
-                along(r).start()
+                o_send[r, rows] = (go_v[rows, r, :].astype(jnp.float32) + branch).astype(jnp.bfloat16)
+                along(r, part, rows).start()
 
     for p in range(phases):
         attention(p)
-        if p == 1:
-            loads[6].wait()
-        if p >= 1:
-            project(p - 1)
-    if phases == 1:
-        loads[6].wait()
-    project(phases - 1)
+    loads[6].wait()
+    for p in range(phases):
+        for part, rows in pieces(p):
+            project(p, part, rows)
     for r in range(recs):
-        along(r).wait_recv()
-        o32[:, r, :] = o_recv[r].astype(jnp.float32)
-    out[...] = o32[...].astype(jnp.bfloat16)
+        for part, rows in pieces(whole_at(r)):
+            along(r, part, rows).wait_recv()
+            o32[rows, r, :] = o_recv[r, rows].astype(jnp.float32)
+            if r == recs - 1:
+                out[rows] = o32[rows].astype(jnp.bfloat16)
     for p in range(phases):
-        for copy in forward(p) + forward_grad(p) + back(p):
+        for copy in forward(p) + forward_grad(p):
             copy.wait_send()
+        for part, rows in pieces(p):
+            for copy in back(p, part, rows):
+                copy.wait_send()
     for r in range(recs):
-        along(r).wait_send()
+        for part, rows in pieces(whole_at(r)):
+            along(r, part, rows).wait_send()
 
 
 def per_device_fused(
@@ -379,9 +395,11 @@
         pltpu.VMEM((recs, frames, width), bf16),
         pltpu.VMEM((frames, recs, width), f32),
         pltpu.SemaphoreType.DMA((7,)),
-        pairs, pairs, pairs, pairs, pairs, pairs,
-        pltpu.SemaphoreType.DMA((recs,)),
-        pltpu.SemaphoreType.DMA((recs,)),
+        pairs, pairs, pairs, pairs,
+        pltpu.SemaphoreType.DMA((phases, 2, n - 1)),
+        pltpu.SemaphoreType.DMA((phases, 2, n - 1)),
+        pltpu.SemaphoreType.DMA((recs, 2)),
+        pltpu.SemaphoreType.DMA((recs, 2)),
     ]
     passed = pl.pallas_call(
         functools.partial(fused_kernel, n, pipes, frames, recs, width, inner),
@@ -390,7 +408,7 @@
         out_specs=vmem,
         scratch_shapes=scratch,
         compiler_params=pltpu.CompilerParams(
-            collective_id=0, has_side_effects=True, vmem_limit_bytes=52 * 1024 * 1024
+            collective_id=0, has_side_effects=True, vmem_limit_bytes=63 * 1024 * 1024
         ),
         cost_estimate=pl.CostEstimate(
             flops=8 * frames * recs * width * inner, bytes_accessed=8 * width * inner, transcendentals=0
@@ -413,7 +431,7 @@
     inner = out_weight.shape[1]
     fits = (
         inner % UNIT == 0 and (recs * (inner // UNIT)) % n == 0 and n > 1 and pipes > 2
-        and frames % 16 == 0 and n * frames <= 256 and recs == 2
+        and frames % 32 == 0 and n * frames <= 256 and recs == 2
     )
     return per_device_fused(*args) if fits else per_device(*args)
 

time: 53.1 us -> 47.3 us (0.89)
  local copies, waits for them, and re-layouts: 6.86 us -> 2.01 us
  Pallas kernels: 45.9 us -> 45 us
    unnamed x15 -> x1, local copies, waits for them, and re-layouts: 6.86 us -> 2.01 us
    pallas_call x1, Pallas kernels: 45.9 us -> 45 us  [per_device_fused(): pl.pallas_call(functools.partial(fused_kernel, n, pipes, frames, recs, wi...]
where the time goes in v3:
time: 47.3 us; the launch traced here: 47.1 us
  Pallas kernels  45 us (95%)
  local copies, waits for them, and re-layouts  2.01 us (4%)
    pallas_call x1, Pallas kernels, per_device_fused(): pl.pallas_call(functools.partial(fused_kernel, n, pipes, frames, recs, wi...  45 us
    unnamed x1, local copies, waits for them, and re-layouts  2.01 us

profile of v3, /device:TPU:1, one launch (start us, length us, event | category | flops | bytes accessed | tf_op | source)
XLA Modules:
  0.0 47.1 jit_solution(18062603105588940079)
XLA Ops:
  0.0 45.0 %shard_map.91 = bf16[64,2,1536]{2,1,0:T(2,128)(2,1)} custom-call(s32[2]{0:T(128)} %bitcast.17, bf16[1,1536]{1,0:T(2,128)(2,1)} %gain.1, bf16[64,2,768]{2,1,0:T(2,128)(2,1)} %bitcast.14, bf16[64,2,768]{2,1,0:T(2,128)(2,1)} %bitcast.15, bf16[64,2,768]{2,1,0:T(2,128)(2,1)} %bitcast.16, bf16[64,2,1536]{2,1,0:T(2,128)(2,1)} %bitcast.12, ...), custom_call_target="tpu_custom_call" | custom-call | flops 1207959552 | bytes 9437184 | tf_op jit(solution)/shard_map/pallas_call | solution.py:404
  45.0 2.0 %copy.11 = bf16[1,64,2,1536]{3,2,1,0:T(2,128)(2,1)} copy(bf16[1,64,2,1536]{3,2,1,0:T(2,128)(2,1)} %bitcast.11) | data formatting | bytes 786432

commit v4 on v3

--- a/solution.py
+++ b/solution.py
@@ -183,7 +183,7 @@
     lens, gain, q_h, k_h, v_h, go_h, ow_h, li_h, qw_h,
     out,
     q_v, k_v, v_v, go_v, ow_v, li_v, qw_v, g32, st, stg, rx, rxg, rs, jn, acc, normed, inv,
-    o_send, o_recv, o32,
+    o_send,
     load_sem, fs, fr, gs, gr, bs, br, ps, pr,
 ):
     seq, pipe = lax.axis_index("seq"), lax.axis_index("pipe")
@@ -245,7 +245,7 @@
 
     def along(r, part, rows):
         return send(
-            o_send.at[r, rows], o_recv.at[r, rows], ps.at[r, part], pr.at[r, part], (before, seq)
+            o_send.at[r, rows], out.at[r, rows], ps.at[r, part], pr.at[r, part], (before, seq)
         )
 
     def start(copies):
@@ -347,9 +347,6 @@
     for r in range(recs):
         for part, rows in pieces(whole_at(r)):
             along(r, part, rows).wait_recv()
-            o32[rows, r, :] = o_recv[r, rows].astype(jnp.float32)
-            if r == recs - 1:
-                out[rows] = o32[rows].astype(jnp.bfloat16)
     for p in range(phases):
         for copy in forward(p) + forward_grad(p):
             copy.wait_send()
@@ -392,8 +389,6 @@
         pltpu.VMEM((recs, frames, width), f32),
         pltpu.VMEM((recs, frames, 128), f32),
         pltpu.VMEM((recs, frames, width), bf16),
-        pltpu.VMEM((recs, frames, width), bf16),
-        pltpu.VMEM((frames, recs, width), f32),
         pltpu.SemaphoreType.DMA((7,)),
         pairs, pairs, pairs, pairs,
         pltpu.SemaphoreType.DMA((phases, 2, n - 1)),
@@ -403,9 +398,9 @@
     ]
     passed = pl.pallas_call(
         functools.partial(fused_kernel, n, pipes, frames, recs, width, inner),
-        out_shape=jax.ShapeDtypeStruct((frames, recs, width), bf16),
+        out_shape=jax.ShapeDtypeStruct((recs, frames, width), bf16),
         in_specs=[pl.BlockSpec(memory_space=pltpu.SMEM), vmem] + [hbm] * 7,
-        out_specs=vmem,
+        out_specs=hbm,
         scratch_shapes=scratch,
         compiler_params=pltpu.CompilerParams(
             collective_id=0, has_side_effects=True, vmem_limit_bytes=63 * 1024 * 1024
@@ -417,7 +412,7 @@
         lengths[0], ln_gain, queries[0], keys_saved[0], values_saved[0], grad_out[0], out_weight[0],
         layer_input[0], qkv_weight[0],
     )
-    return passed[None]
+    return jnp.transpose(passed, (1, 0, 2))[None]
 
 
 def body_for(

time: 47.3 us -> 46.6 us (0.985)
  Pallas kernels: 45 us -> 44.2 us
    broadcast_in_dim x0 -> x1, local copies, waits for them, and re-layouts: none -> 2.15 us  [per_device_fused(): return jnp.transpose(passed, (1, 0, 2))[None]]
    unnamed x1 -> x0, local copies, waits for them, and re-layouts: 2.01 us -> none
    pallas_call x1, Pallas kernels: 45 us -> 44.2 us  [per_device_fused(): pl.pallas_call(functools.partial(fused_kernel, n, pipes, frames, recs, wi...]
where the time goes in v4:
time: 46.6 us; the launch traced here: 46.4 us
  Pallas kernels  44.2 us (95%)
  local copies, waits for them, and re-layouts  2.15 us (5%)
    pallas_call x1, Pallas kernels, per_device_fused(): pl.pallas_call(functools.partial(fused_kernel, n, pipes, frames, recs, wi...  44.2 us
    broadcast_in_dim x1, local copies, waits for them, and re-layouts, per_device_fused(): return jnp.transpose(passed, (1, 0, 2))[None]  2.15 us

profile of v4, /device:TPU:1, one launch (start us, length us, event | category | flops | bytes accessed | tf_op | source)
XLA Modules:
  0.0 46.4 jit_solution(2916422044660071831)
XLA Ops:
  0.0 44.2 %shard_map.91 = bf16[2,64,1536]{2,1,0:T(8,128)(2,1)} custom-call(s32[2]{0:T(128)} %bitcast.19, bf16[1,1536]{1,0:T(2,128)(2,1)} %gain.1, bf16[64,2,768]{2,1,0:T(2,128)(2,1)} %bitcast.16, bf16[64,2,768]{2,1,0:T(2,128)(2,1)} %bitcast.17, bf16[64,2,768]{2,1,0:T(2,128)(2,1)} %bitcast.18, bf16[64,2,1536]{2,1,0:T(2,128)(2,1)} %bitcast.14, ...), custom_call_target="tpu_custom_call" | custom-call | flops 1207959552 | bytes 9437184 | tf_op jit(solution)/shard_map/pallas_call | solution.py:399
  44.2 2.1 %copy.10 = bf16[1,64,2,1536]{3,2,1,0:T(2,128)(2,1)} copy(bf16[1,64,2,1536]{3,1,2,0:T(8,128)(2,1)} %bitcast.13) | data formatting | bytes 786432 | tf_op jit(solution)/shard_map/broadcast_in_dim | solution.py:415
